TPU v7x, 512 devices: a whole 4x8x8 slice. The times are simulated.
512 devices in a mesh: row: 32 (over x, y), col: 16 (over z, core).
Axes of the slice: x: 4, y: 8, z: 8, core: 2. Of those that a mesh axis runs over, the one named last changes fastest.
Arguments:
- points: bfloat16 [32, 65536], P(None, ('row', 'col')), may hold values from -6 to 6
- inv_scale: float32 [32], replicated, may hold values from 0.3 to 0.6
- amplitude: float32 [1], replicated, may hold values from 0.5 to 1.5
- noise: float32 [65536], P(('row', 'col')), may hold values from 0.1 to 4.2
- targets: float32 [65536], P(('row', 'col')), may hold values from -6 to 6
- probe_seeds: int32 [65536], P(('row', 'col')), may hold values from 0 to 127
Outputs:
- solution: float32 [8, 65536], P(None, ('row', 'col'))
- residual: float32 [8, 65536], P(None, ('row', 'col'))
All inputs are finite; a program needn't handle non-finite values.
Results may differ from a plain program's by a relative error of at most 0.0097.
Values may be sent and summed in bfloat16 or wider, within the bound.
A program may use at most 64 MiB of HBM per device.

v0:
```python
import math

import jax
import jax.numpy as jnp
from jax import lax
from jax.sharding import PartitionSpec as P

RHS = 8
ITERS = 2


def shifted(value, axis, steps):
    count = lax.axis_size(axis)
    pairs = [(source, (source + steps) % count) for source in range(count)]
    return lax.ppermute(value, axis, pairs)


def kernel_tile(row_points, row_norms, col_points, col_norms):
    products = lax.dot_general(
        row_points, col_points, (((0,), (0,)), ((), ())), preferred_element_type=jnp.float32
    )
    return jnp.exp(products - 0.5 * row_norms[:, None] - 0.5 * col_norms[None, :]).astype(
        jnp.bfloat16
    )


def square_norms(values_bf):
    values = values_bf.astype(jnp.float32)
    return jnp.sum(values * values, axis=0)


def build_rhs(targets, probe_seeds):
    powers = (2 ** jnp.arange(RHS - 1)).astype(jnp.int32)
    flags = probe_seeds[None, :] // powers[:, None] % 2
    probes = (1 - 2 * flags).astype(jnp.float32)
    return jnp.concatenate([targets[None, :], probes], axis=0)


def forward_only(row_points, row_norms, col_points, col_norms, col_dirs):
    rows = row_points.shape[1]
    height = math.gcd(rows, 512)

    def forward_visit(index, result):
        start = index * height
        slab = lax.dynamic_slice_in_dim(row_points, start, height, 1)
        slab_norms = lax.dynamic_slice_in_dim(row_norms, start, height, 0)
        tile = kernel_tile(slab, slab_norms, col_points, col_norms)
        part = lax.dot_general(
            col_dirs, tile, (((1,), (1,)), ((), ())), preferred_element_type=jnp.float32
        )
        return lax.dynamic_update_slice_in_dim(result, part, start, 1)

    empty = jnp.zeros((col_dirs.shape[0], rows), jnp.float32)
    return lax.fori_loop(0, rows // height, forward_visit, empty)


def both_ways(row_points, row_norms, row_dirs, col_points, col_norms, col_dirs):
    rows = row_points.shape[1]
    height = math.gcd(rows, 512)

    def both_visit(index, carry):
        forward, mirror = carry
        start = index * height
        slab = lax.dynamic_slice_in_dim(row_points, start, height, 1)
        slab_norms = lax.dynamic_slice_in_dim(row_norms, start, height, 0)
        slab_dirs = lax.dynamic_slice_in_dim(row_dirs, start, height, 1)
        tile = kernel_tile(slab, slab_norms, col_points, col_norms)
        part = lax.dot_general(
            col_dirs, tile, (((1,), (1,)), ((), ())), preferred_element_type=jnp.float32
        )
        forward = lax.dynamic_update_slice_in_dim(forward, part, start, 1)
        mirror = mirror + jnp.dot(slab_dirs, tile, preferred_element_type=jnp.float32)
        return (forward, mirror)

    start_forward = jnp.zeros((col_dirs.shape[0], rows), jnp.float32)
    start_mirror = jnp.zeros((col_dirs.shape[0], col_points.shape[1]), jnp.float32)
    return lax.fori_loop(0, rows // height, both_visit, (start_forward, start_mirror))


def fetch_points(block, offset, levels):
    for level in range(levels):
        moved = shifted(block, "row", -(1 << level))
        block = jnp.where(offset // (1 << level) % 2 == 1, moved, block)
    return block


def fetch_directions(block, offset, levels):
    for level in range(levels):
        moved = shifted(block, "row", -(1 << level))
        block = jnp.where(offset // (1 << level) % 2 == 1, moved, block)
    return block


def return_mirror(block, offset, levels):
    for level in range(levels):
        moved = shifted(block.astype(jnp.bfloat16), "row", 1 << level).astype(block.dtype)
        block = jnp.where(offset // (1 << level) % 2 == 1, moved, block)
    return block


def squares(residual):
    return lax.psum(jnp.sum(residual * residual, axis=1), ("row", "col"))


def shards(points, inv_scale, amplitude, noise, targets, probe_seeds):
    scaled = (points.astype(jnp.float32) * inv_scale[:, None]).astype(jnp.bfloat16)
    block_points = lax.all_gather(scaled, "col", axis=1, tiled=True)
    block_norms = square_norms(block_points)
    row_count = lax.axis_size("row")
    col_count = lax.axis_size("col")
    levels = row_count.bit_length() - 1
    col_index = lax.axis_index("col")
    offset = col_index + 1
    mirror_weight = jnp.where(offset < col_count, 1.0, 0.0).astype(jnp.float32)
    partner_points = fetch_points(block_points, offset, levels)
    partner_norms = square_norms(partner_points)
    rhs = build_rhs(targets, probe_seeds)
    solution = jnp.zeros_like(rhs)
    residual = rhs
    direction = rhs
    norm_now = squares(residual)
    for step in range(ITERS):
        low = direction.astype(jnp.bfloat16)
        low_values = low.astype(jnp.float32)
        block_dirs = lax.all_gather(low, "col", axis=1, tiled=True)
        partner_dirs = fetch_directions(block_dirs, offset, levels)
        forward, mirror = both_ways(
            block_points, block_norms, block_dirs, partner_points, partner_norms, partner_dirs
        )
        mirror = mirror * mirror_weight
        extra = lax.cond(
            col_index == 0,
            lambda: forward_only(block_points, block_norms, block_points, block_norms, block_dirs),
            lambda: jnp.zeros_like(forward),
        )
        forward = forward + extra
        arrived = return_mirror(mirror, offset, levels)
        reduced = lax.psum_scatter(forward + arrived, "col", scatter_dimension=1, tiled=True)
        image = amplitude[0] * reduced + noise[None, :] * low_values
        local_curve = jnp.sum(low_values * image, axis=1)
        curvature = lax.psum(local_curve, ("row", "col"))
        alpha = norm_now / curvature
        solution = solution + alpha[:, None] * direction
        residual = residual - alpha[:, None] * image
        if step + 1 < ITERS:
            norm_next = squares(residual)
            direction = residual + (norm_next / norm_now)[:, None] * direction
            norm_now = norm_next
    return (solution, residual)


def solution(mesh):
    placed = (
        P(None, ("row", "col")),
        P(),
        P(),
        P(("row", "col")),
        P(("row", "col")),
        P(("row", "col")),
    )
    return jax.shard_map(
        shards,
        mesh=mesh,
        in_specs=placed,
        out_specs=(P(None, ("row", "col")), P(None, ("row", "col"))),
        check_vma=False,
    )
```

profile of v0, /device:TPU:1, one launch (start us, length us, event | category | flops | bytes accessed | tf_op | source)
XLA Modules:
  0.0 682.5 jit_solution(10187556886131814006)
XLA Ops:
  7.9 0.9 fusion.37
  9.4 24.5 %all_gather.10 = bf16[8,2048]{1,0:T(8,128)(2,1)S(1)} all-gather(bf16[8,128]{1,0:T(8,128)(2,1)S(1)} %fusion.42), channel_id=1, replica_groups=mesh['row'=32,'col'=16] {'col'}, dimensions={1}, use_global_device_ids=true | all-gather | bytes 34816 | tf_op jit(solution)/shard_map/all_gather | solution.py:125
  34.0 7.3 %collective-permute-start.5 = (bf16[8,2048]{1,0:T(8,128)(2,1)S(1)}, bf16[8,2048]{1,0:T(8,128)(2,1)S(1)}, u32[]{:S(2)}, u32[]{:S(2)}) collective-permute-start(bf16[8,2048]{1,0:T(8,128)(2,1)S(1)} %all_gather.10), channel_id=1, source_target_pairs={{0,496},{16,0},{32,16},{48,32},{64,48},{80,64},{96,80},{112,96},{1... | collective-permute-start | bytes 98312 | tf_op jit(solution)/shard_map/ppermute | solution.py:15
  42.0 14.8 %all_gather.9 = bf16[32,2048]{1,0:T(8,128)(2,1)S(1)} all-gather(bf16[32,128]{1,0:T(8,128)(2,1)S(1)} %multiply_convert_fusion.2), channel_id=1, replica_groups=mesh['row'=32,'col'=16] {'col'}, dimensions={1}, use_global_device_ids=true | all-gather | bytes 139264 | tf_op jit(solution)/shard_map/all_gather | solution.py:107
  56.8 3.0 collective-permute-start
  60.0 3.8 collective-permute-start.6
  63.8 3.6 collective-permute-start.1
  67.5 4.3 collective-permute-start.7
  71.7 3.0 collective-permute-done.1
  74.8 2.2 collective-permute-start.2
  77.0 2.2 collective-permute-start.8
  79.2 6.5 collective-permute-done.2
  85.7 1.9 collective-permute-start.3
  87.7 4.3 collective-permute-start.9
  92.1 3.0 collective-permute-start.4
  95.1 4.2 collective-permute-done.4
  99.4 7.9 %while.58 = (s32[]{:T(128)}, f32[8,2048]{1,0:T(8,128)S(1)}, f32[8,2048]{1,0:T(8,128)S(1)}, bf16[32,2048]{1,0:T(8,128)(2,1)S(1)}, bf16[32,2048]{1,0:T(8,128)(2,1)...) while((s32[]{:T(128)}, f32[8,2048]{1,0:T(8,128)S(1)}, ...), condition=%wide.region_5.6_spmd.clone, body=%wide.region_4.5_spmd.clone.sunk | while | flops 103844360 | bytes 6674629 | solution.py:77
  101.4 0.9 exponential_convert_fusion.6
  103.4 0.9 exponential_convert_fusion.6
  105.4 0.9 exponential_convert_fusion.6
  107.3 4.1 collective-permute-start.10
  111.4 10.3 %collective-permute-done.10 = bf16[8,2048]{1,0:T(8,128)(2,1)S(1)} collective-permute-done((bf16[8,2048]{1,0:T(8,128)(2,1)S(1)}, bf16[8,2048]{1,0:T(8,128)(2,1)S(1)}, u32[]{:S(2)}, u32[]{:S(2)}) %collective-permute-start.10) | collective-permute-done | bytes 32800 | tf_op jit(solution)/shard_map/ppermute | solution.py:15
  121.7 1.9 collective-permute-start.11
  123.6 6.9 %collective-permute-done.11 = bf16[8,2048]{1,0:T(8,128)(2,1)S(1)} collective-permute-done((bf16[8,2048]{1,0:T(8,128)(2,1)S(1)}, bf16[8,2048]{1,0:T(8,128)(2,1)S(1)}, u32[]{:S(2)}, u32[]{:S(2)}) %collective-permute-start.11) | collective-permute-done | bytes 32800 | tf_op jit(solution)/shard_map/ppermute | solution.py:15
  130.6 1.9 collective-permute-start.12
  132.5 8.8 %collective-permute-done.12 = bf16[8,2048]{1,0:T(8,128)(2,1)S(1)} collective-permute-done((bf16[8,2048]{1,0:T(8,128)(2,1)S(1)}, bf16[8,2048]{1,0:T(8,128)(2,1)S(1)}, u32[]{:S(2)}, u32[]{:S(2)}) %collective-permute-start.12) | collective-permute-done | bytes 32800 | tf_op jit(solution)/shard_map/ppermute | solution.py:15
  141.3 1.9 collective-permute-start.13
  143.3 4.1 collective-permute-done.13
  147.4 1.9 collective-permute-start.14
  150.0 3.6 collective-permute-done.14
  153.6 1.5 select_add_fusion.1
  155.9 58.2 %reduce-scatter.3.cloned.1.call-done = f32[8,128]{1,0:T(8,128)} async-done(((f32[8,2048]{1,0:T(8,128)}), f32[8,128]{1,0:T(8,128)}) %reduce-scatter.3.cloned.1.call-update) | async-done | bytes 4112 | tf_op jit(solution)/shard_map/reduce_scatter | solution.py:138
  214.9 99.8 %all-reduce = (f32[8]{0:T(128)S(1)}, f32[8]{0:T(128)S(1)}) all-reduce(f32[8]{0:T(128)S(1)} %multiply_reduce_fusion.3, f32[8]{0:T(128)S(1)} %fusion.31), channel_id=1, replica_groups=mesh['row'=32,'col'=16] {'row','col'}, use_global_device_ids=true, to_apply=%region_1.2 | all-reduce | flops 16 | bytes 128 | tf_op jit(solution)/shard_map/psum | solution.py:102
  314.7 0.9 multiply_reduce_fusion.2
  315.6 94.4 %psum.30 = f32[8]{0:T(128)S(1)} all-reduce(f32[8]{0:T(128)S(1)} %get-tuple-element.648), channel_id=1, replica_groups=mesh['row'=32,'col'=16] {'row','col'}, use_global_device_ids=true, to_apply=%region_14.15 | all-reduce | flops 8 | bytes 64 | tf_op jit(solution)/shard_map/psum | solution.py:102
  410.1 16.2 %all_gather.11 = bf16[8,2048]{1,0:T(8,128)(2,1)S(1)} all-gather(bf16[8,128]{1,0:T(8,128)(2,1)S(1)} %fusion.39), channel_id=1, replica_groups=mesh['row'=32,'col'=16] {'col'}, dimensions={1}, use_global_device_ids=true | all-gather | bytes 34816 | tf_op jit(solution)/shard_map/all_gather | solution.py:125
  426.2 3.6 collective-permute-start.15
  429.9 1.0 collective-permute-done.15
  430.9 5.4 collective-permute-start.16
  436.3 1.0 collective-permute-done.16
  437.3 6.3 collective-permute-start.17
  443.6 2.3 collective-permute-done.17
  445.9 2.8 collective-permute-start.18
  448.7 1.8 collective-permute-done.18
  450.6 3.7 collective-permute-start.19
  454.3 2.5 collective-permute-done.19
  456.7 7.9 %while.59 = (s32[]{:T(128)}, f32[8,2048]{1,0:T(8,128)S(1)}, f32[8,2048]{1,0:T(8,128)S(1)}, bf16[32,2048]{1,0:T(8,128)(2,1)S(1)}, bf16[32,2048]{1,0:T(8,128)(2,1)...) while((s32[]{:T(128)}, f32[8,2048]{1,0:T(8,128)S(1)}, ...), condition=%wide.region_16.17_spmd.clone, body=%wide.region_15.16_spmd.clone.sunk | while | flops 103844360 | bytes 6674629 | solution.py:77
  458.8 0.9 exponential_convert_fusion.7
  460.8 0.9 exponential_convert_fusion.7
  462.8 0.9 exponential_convert_fusion.7
  464.7 4.6 collective-permute-start.20
  469.3 9.7 %collective-permute-done.20 = bf16[8,2048]{1,0:T(8,128)(2,1)S(1)} collective-permute-done((bf16[8,2048]{1,0:T(8,128)(2,1)S(1)}, bf16[8,2048]{1,0:T(8,128)(2,1)S(1)}, u32[]{:S(2)}, u32[]{:S(2)}) %collective-permute-start.20) | collective-permute-done | bytes 32800 | tf_op jit(solution)/shard_map/ppermute | solution.py:15
  479.1 1.9 collective-permute-start.21
  481.0 6.9 %collective-permute-done.21 = bf16[8,2048]{1,0:T(8,128)(2,1)S(1)} collective-permute-done((bf16[8,2048]{1,0:T(8,128)(2,1)S(1)}, bf16[8,2048]{1,0:T(8,128)(2,1)S(1)}, u32[]{:S(2)}, u32[]{:S(2)}) %collective-permute-start.21) | collective-permute-done | bytes 32800 | tf_op jit(solution)/shard_map/ppermute | solution.py:15
  488.0 1.9 collective-permute-start.22
  489.9 8.7 %collective-permute-done.22 = bf16[8,2048]{1,0:T(8,128)(2,1)S(1)} collective-permute-done((bf16[8,2048]{1,0:T(8,128)(2,1)S(1)}, bf16[8,2048]{1,0:T(8,128)(2,1)S(1)}, u32[]{:S(2)}, u32[]{:S(2)}) %collective-permute-start.22) | collective-permute-done | bytes 32800 | tf_op jit(solution)/shard_map/ppermute | solution.py:15
  498.7 1.9 collective-permute-start.23
  500.6 4.2 collective-permute-done.23
  504.8 1.9 collective-permute-start.24
  507.4 3.6 collective-permute-done.24
  511.0 1.5 select_add_fusion
  512.5 61.3 %reduce-scatter.5.cloned.1.call-done = f32[8,128]{1,0:T(8,128)} async-done(((f32[8,2048]{1,0:T(8,128)}), f32[8,128]{1,0:T(8,128)}) %reduce-scatter.5.cloned.1.call-update) | async-done | bytes 4112 | tf_op jit(solution)/shard_map/reduce_scatter | solution.py:138
  574.6 99.7 %psum.31 = f32[8]{0:T(128)S(1)} all-reduce(f32[8]{0:T(128)S(1)} %fusion.33), channel_id=1, replica_groups=mesh['row'=32,'col'=16] {'row','col'}, use_global_device_ids=true, to_apply=%region_23.24 | all-reduce | flops 8 | bytes 64 | tf_op jit(solution)/shard_map/psum | solution.py:141
  674.3 1.4 multiply_subtract_fusion
  (94 shorter events, 17.6 us)
Async XLA Ops:
  7.2 207.0 %reduce-scatter.3.cloned.1.call-start = ((), (), s32[]{:S(2)}) async-start(), calls=%async_computation.2 | async-start | bytes 69632 | tf_op jit(solution)/shard_map/reduce_scatter | solution.py:138
  34.0 26.0 %collective-permute-start.5 = (bf16[8,2048]{1,0:T(8,128)(2,1)S(1)}, bf16[8,2048]{1,0:T(8,128)(2,1)S(1)}, u32[]{:S(2)}, u32[]{:S(2)}) collective-permute-start(bf16[8,2048]{1,0:T(8,128)(2,1)S(1)} %all_gather.10), channel_id=1, source_target_pairs={{0,496},{16,0},{32,16},{48,32},{64,48},{80,64},{96,80},{112,96},{1... | collective-permute-start | bytes 98312 | tf_op jit(solution)/shard_map/ppermute | solution.py:15
  56.8 7.0 %collective-permute-start = (bf16[32,2048]{1,0:T(8,128)(2,1)S(1)}, bf16[32,2048]{1,0:T(8,128)(2,1)S(1)}, u32[]{:S(2)}, u32[]{:S(2)}) collective-permute-start(bf16[32,2048]{1,0:T(8,128)(2,1)S(1)} %all_gather.9), channel_id=1, source_target_pairs={{0,496},{16,0},{32,16},{48,32},{64,48},{80,64},{96,80},{112,96},{1... | collective-permute-start | bytes 393224 | tf_op jit(solution)/shard_map/ppermute | solution.py:15
  60.0 7.4 %collective-permute-start.6 = (bf16[8,2048]{1,0:T(8,128)(2,1)S(1)}, bf16[8,2048]{1,0:T(8,128)(2,1)S(1)}, u32[]{:S(2)}, u32[]{:S(2)}) collective-permute-start(bf16[8,2048]{1,0:T(8,128)(2,1)S(1)} %broadcast_select_fusion.6), channel_id=1, source_target_pairs={{0,480},{16,496},{32,0},{48,16},{64,32},{80,48},{96,64},{112,80},{... | collective-permute-start | bytes 98312 | tf_op jit(solution)/shard_map/ppermute | solution.py:15
  63.8 10.9 %collective-permute-start.1 = (bf16[32,2048]{1,0:T(8,128)(2,1)S(1)}, bf16[32,2048]{1,0:T(8,128)(2,1)S(1)}, u32[]{:S(2)}, u32[]{:S(2)}) collective-permute-start(bf16[32,2048]{1,0:T(8,128)(2,1)S(1)} %broadcast_select_fusion), channel_id=1, source_target_pairs={{0,480},{16,496},{32,0},{48,16},{64,32},{80,48},{96,64},{112,80},{... | collective-permute-start | bytes 393224 | tf_op jit(solution)/shard_map/ppermute | solution.py:15
  67.5 9.5 %collective-permute-start.7 = (bf16[8,2048]{1,0:T(8,128)(2,1)S(1)}, bf16[8,2048]{1,0:T(8,128)(2,1)S(1)}, u32[]{:S(2)}, u32[]{:S(2)}) collective-permute-start(bf16[8,2048]{1,0:T(8,128)(2,1)S(1)} %broadcast_select_fusion.8), channel_id=1, source_target_pairs={{0,448},{16,464},{32,480},{48,496},{64,0},{80,16},{96,32},{112,48}... | collective-permute-start | bytes 98312 | tf_op jit(solution)/shard_map/ppermute | solution.py:15
  74.8 10.9 %collective-permute-start.2 = (bf16[32,2048]{1,0:T(8,128)(2,1)S(1)}, bf16[32,2048]{1,0:T(8,128)(2,1)S(1)}, u32[]{:S(2)}, u32[]{:S(2)}) collective-permute-start(bf16[32,2048]{1,0:T(8,128)(2,1)S(1)} %broadcast_select_fusion.1), channel_id=1, source_target_pairs={{0,448},{16,464},{32,480},{48,496},{64,0},{80,16},{96,32},{112,48}... | collective-permute-start | bytes 393224 | tf_op jit(solution)/shard_map/ppermute | solution.py:15
  77.0 10.7 %collective-permute-start.8 = (bf16[8,2048]{1,0:T(8,128)(2,1)S(1)}, bf16[8,2048]{1,0:T(8,128)(2,1)S(1)}, u32[]{:S(2)}, u32[]{:S(2)}) collective-permute-start(bf16[8,2048]{1,0:T(8,128)(2,1)S(1)} %broadcast_select_fusion.10), channel_id=1, source_target_pairs={{0,384},{16,400},{32,416},{48,432},{64,448},{80,464},{96,480},{112... | collective-permute-start | bytes 98312 | tf_op jit(solution)/shard_map/ppermute | solution.py:15
  85.7 6.3 collective-permute-start.3
  87.7 7.4 %collective-permute-start.9 = (bf16[8,2048]{1,0:T(8,128)(2,1)S(1)}, bf16[8,2048]{1,0:T(8,128)(2,1)S(1)}, u32[]{:S(2)}, u32[]{:S(2)}) collective-permute-start(bf16[8,2048]{1,0:T(8,128)(2,1)S(1)} %broadcast_select_fusion.12), channel_id=1, source_target_pairs={{0,256},{16,272},{32,288},{48,304},{64,320},{80,336},{96,352},{112... | collective-permute-start | bytes 98312 | tf_op jit(solution)/shard_map/ppermute | solution.py:15
  92.1 7.2 %collective-permute-start.4 = (bf16[32,2048]{1,0:T(8,128)(2,1)S(1)}, bf16[32,2048]{1,0:T(8,128)(2,1)S(1)}, u32[]{:S(2)}, u32[]{:S(2)}) collective-permute-start(bf16[32,2048]{1,0:T(8,128)(2,1)S(1)} %broadcast_select_fusion.3), channel_id=1, source_target_pairs={{0,256},{16,272},{32,288},{48,304},{64,320},{80,336},{96,352},{112... | collective-permute-start | bytes 393224 | tf_op jit(solution)/shard_map/ppermute | solution.py:15
  107.3 14.4 %collective-permute-start.10 = (bf16[8,2048]{1,0:T(8,128)(2,1)S(1)}, bf16[8,2048]{1,0:T(8,128)(2,1)S(1)}, u32[]{:S(2)}, u32[]{:S(2)}) collective-permute-start(bf16[8,2048]{1,0:T(8,128)(2,1)S(1)} %multiply_convert_fusion.1), channel_id=1, source_target_pairs={{0,16},{16,32},{32,48},{48,64},{64,80},{80,96},{96,112},{112,128},... | collective-permute-start | bytes 98312 | tf_op jit(solution)/shard_map/ppermute | solution.py:15
  121.7 8.9 %collective-permute-start.11 = (bf16[8,2048]{1,0:T(8,128)(2,1)S(1)}, bf16[8,2048]{1,0:T(8,128)(2,1)S(1)}, u32[]{:S(2)}, u32[]{:S(2)}) collective-permute-start(bf16[8,2048]{1,0:T(8,128)(2,1)S(1)} %fusion.28), channel_id=1, source_target_pairs={{0,32},{16,48},{32,64},{48,80},{64,96},{80,112},{96,128},{112,144}... | collective-permute-start | bytes 98312 | tf_op jit(solution)/shard_map/ppermute | solution.py:15
  130.6 10.7 %collective-permute-start.12 = (bf16[8,2048]{1,0:T(8,128)(2,1)S(1)}, bf16[8,2048]{1,0:T(8,128)(2,1)S(1)}, u32[]{:S(2)}, u32[]{:S(2)}) collective-permute-start(bf16[8,2048]{1,0:T(8,128)(2,1)S(1)} %fusion.24), channel_id=1, source_target_pairs={{0,64},{16,80},{32,96},{48,112},{64,128},{80,144},{96,160},{112,17... | collective-permute-start | bytes 98312 | tf_op jit(solution)/shard_map/ppermute | solution.py:15
  141.3 6.1 collective-permute-start.13
  147.4 6.2 collective-permute-start.14
  149.3 6.4 copy-start
  149.4 64.8 %copy-start.1 = (f32[128]{0:T(128)S(1)}, f32[128]{0:T(128)}, u32[]{:S(2)}) copy-start(f32[128]{0:T(128)} %param.21) | copy-start | bytes 1540
  155.1 418.7 %reduce-scatter.5.cloned.1.call-start = ((), (), s32[]{:S(2)}) async-start(), calls=%async_computation.3 | async-start | bytes 69632 | tf_op jit(solution)/shard_map/reduce_scatter | solution.py:138
  426.2 4.7 collective-permute-start.15
  430.9 6.4 collective-permute-start.16
  437.3 8.6 %collective-permute-start.17 = (bf16[8,2048]{1,0:T(8,128)(2,1)S(1)}, bf16[8,2048]{1,0:T(8,128)(2,1)S(1)}, u32[]{:S(2)}, u32[]{:S(2)}) collective-permute-start(bf16[8,2048]{1,0:T(8,128)(2,1)S(1)} %broadcast_select_fusion.7), channel_id=1, source_target_pairs={{0,448},{16,464},{32,480},{48,496},{64,0},{80,16},{96,32},{112,48}... | collective-permute-start | bytes 98312 | tf_op jit(solution)/shard_map/ppermute | solution.py:15
  445.9 4.7 collective-permute-start.18
  450.6 6.2 collective-permute-start.19
  464.7 14.3 %collective-permute-start.20 = (bf16[8,2048]{1,0:T(8,128)(2,1)S(1)}, bf16[8,2048]{1,0:T(8,128)(2,1)S(1)}, u32[]{:S(2)}, u32[]{:S(2)}) collective-permute-start(bf16[8,2048]{1,0:T(8,128)(2,1)S(1)} %multiply_convert_fusion), channel_id=1, source_target_pairs={{0,16},{16,32},{32,48},{48,64},{64,80},{80,96},{96,112},{112,128},... | collective-permute-start | bytes 98312 | tf_op jit(solution)/shard_map/ppermute | solution.py:15
  479.1 8.9 %collective-permute-start.21 = (bf16[8,2048]{1,0:T(8,128)(2,1)S(1)}, bf16[8,2048]{1,0:T(8,128)(2,1)S(1)}, u32[]{:S(2)}, u32[]{:S(2)}) collective-permute-start(bf16[8,2048]{1,0:T(8,128)(2,1)S(1)} %fusion.29), channel_id=1, source_target_pairs={{0,32},{16,48},{32,64},{48,80},{64,96},{80,112},{96,128},{112,144}... | collective-permute-start | bytes 98312 | tf_op jit(solution)/shard_map/ppermute | solution.py:15
  488.0 10.7 %collective-permute-start.22 = (bf16[8,2048]{1,0:T(8,128)(2,1)S(1)}, bf16[8,2048]{1,0:T(8,128)(2,1)S(1)}, u32[]{:S(2)}, u32[]{:S(2)}) collective-permute-start(bf16[8,2048]{1,0:T(8,128)(2,1)S(1)} %fusion.26), channel_id=1, source_target_pairs={{0,64},{16,80},{32,96},{48,112},{64,128},{80,144},{96,160},{112,17... | collective-permute-start | bytes 98312 | tf_op jit(solution)/shard_map/ppermute | solution.py:15
  498.7 6.2 collective-permute-start.23
  504.8 6.2 collective-permute-start.24
Sparse Core Ops, SparseCore 0:
  155.2 58.9 reduce-scatter.2
  512.6 61.0 reduce-scatter.4
where the time goes:
time: 684 us; the launch traced here: 682 us
  blocking collectives  349 us (51%)
  waiting for transfers between devices  209 us (31%)
  starting transfers between devices  81.5 us (12%)
  between operations  15.3 us (2%)
  matrix products  15.1 us (2%)
  other arithmetic  11 us (2%)
    psum x2, blocking collectives, squares(): return lax.psum(jnp.sum(residual * residual, axis=1), ('row', 'col'))  194 us
    reduce_scatter x2, waiting for transfers between devices, shards(): lax.psum_scatter(forward + arrived, 'col', scatter_dimension=1, tiled=True)  120 us
    psum x1, blocking collectives, shards(): curvature = lax.psum(local_curve, ('row', 'col'))  99.7 us
    ppermute x25, waiting for transfers between devices, shifted(): return lax.ppermute(value, axis, pairs)  89.2 us
    ppermute x25, starting transfers between devices, shifted(): return lax.ppermute(value, axis, pairs)  81.5 us
    all_gather x2, blocking collectives, shards(): block_dirs = lax.all_gather(low, 'col', axis=1, tiled=True)  40.7 us
    all_gather x1, blocking collectives, shards(): block_points = lax.all_gather(scaled, 'col', axis=1, tiled=True)  14.8 us
  transfers between devices with their start and end apart: 27, of which 20 were waited for; matrix products, arithmetic and copies ran while one was open for 0% of the time, Pallas kernels for 0%

commit v1 on v0

v1 whole, which is shorter than its diff:
```python
import jax
import jax.numpy as jnp
from jax import lax
from jax.experimental import pallas as pl
from jax.experimental.pallas import tpu as pltpu
from jax.sharding import PartitionSpec as P

MESH = pl.DeviceIdType.MESH
F = 32
RHS = 8
LANES = 128
F32 = jnp.float32
BF16 = jnp.bfloat16

ROWS = 48


def pieces(value):
    first = value.astype(BF16).astype(F32)
    rest = value - first
    second = rest.astype(BF16).astype(F32)
    return first, second, rest - second


def wait_bytes(ref, sem):
    pltpu.make_async_copy(ref, ref, sem).wait()


def body(nx, ny, nc, refs):
    (points, inv, amp, noise, targets, seeds, sol, res) = refs[:8]
    (msg, jbuf, ibuf, weights, tile, acc, rs1, msg2, j2, i2, sc1, scal1,
     send2, rs2, fin_msg, fin) = refs[8:24]
    (s_row, s_col, r_row, r_col, s_rs1, r_rs1, s_row2, s_col2, r_row2, r_col2,
     s_sc, r_sc, s_rs2, r_rs2, s_fin, r_fin) = refs[24:]
    nr = nx * ny
    rows_i = nc * LANES
    group = ny * LANES
    row = lax.axis_index("row")
    col = lax.axis_index("col")
    x = row // ny
    y = row % ny

    def row_peer(k):
        return ((x + k // ny) % nx) * ny + (y + k % ny) % ny

    def col_peer(k):
        return (col + k) % nc

    def to_rows(src, dst, send, recv):
        pltpu.make_async_copy(src, dst, recv).start()

        def go(k, carry):
            pltpu.make_async_remote_copy(
                src_ref=src, dst_ref=dst, send_sem=send, recv_sem=recv,
                device_id=(row_peer(k), col), device_id_type=MESH,
            ).start()
            return carry

        lax.fori_loop(1, nr, go, 0)

    def to_cols(src_of, dst, send, recv):
        pltpu.make_async_copy(src_of(col), dst, recv).start()

        def go(k, carry):
            peer = col_peer(k)
            pltpu.make_async_remote_copy(
                src_ref=src_of(peer), dst_ref=dst, send_sem=send, recv_sem=recv,
                device_id=(row, peer), device_id_type=MESH,
            ).start()
            return carry

        lax.fori_loop(1, nc, go, 0)

    barrier = pltpu.get_barrier_semaphore()

    def greet_row(k, carry):
        pl.semaphore_signal(barrier, inc=1, device_id=(row_peer(k), col), device_id_type=MESH)
        return carry

    def greet_col(k, carry):
        pl.semaphore_signal(barrier, inc=1, device_id=(row, col_peer(k)), device_id_type=MESH)
        return carry

    lax.fori_loop(1, nr, greet_row, 0)
    lax.fori_loop(1, nc, greet_col, 0)

    eye = lax.broadcasted_iota(jnp.int32, (F, F), 0) == lax.broadcasted_iota(jnp.int32, (F, F), 1)
    factor = jnp.sum(jnp.where(eye, inv[...], 0.0), axis=1, keepdims=True)
    scaled = (points[...].astype(F32) * factor).astype(BF16)
    values = scaled.astype(F32)
    norm = -0.5 * jnp.sum(values * values, axis=0, keepdims=True)
    n1, n2, n3 = pieces(norm)
    sub = lax.broadcasted_iota(jnp.int32, (RHS, LANES), 0)
    lane = lax.broadcasted_iota(jnp.int32, (RHS, LANES), 1)
    bits = (seeds[...] >> jnp.maximum(sub - 1, 0)) & 1
    v0 = jnp.where(sub == 0, targets[...], (1 - 2 * bits).astype(F32))
    low = v0.astype(BF16).astype(F32)
    lost = targets[...] - targets[...].astype(BF16).astype(F32)
    extra = jnp.where(sub == 0, n1, jnp.where(sub == 1, n2, jnp.where(sub == 2, n3,
            jnp.where(sub < 6, 1.0, jnp.where(sub == 6, lost, 0.0)))))
    msg[0:F, :] = scaled
    msg[F:ROWS, :] = jnp.concatenate([extra, low], axis=0).astype(BF16)

    pl.semaphore_wait(barrier, nr - 1 + nc - 1)
    to_cols(lambda peer: msg, ibuf.at[col], s_col, r_col)
    to_rows(msg, jbuf.at[row], s_row, r_row.at[x])

    wait_bytes(ibuf, r_col)
    for c in range(nc):
        part = slice(c * LANES, (c + 1) * LANES)
        weights[0:F, part] = ibuf[c, 0:F, :]
        tail = ibuf[c, F:ROWS, :].astype(F32)
        swapped = jnp.where(sub < 3, 1.0, jnp.where(sub < 6, jnp.roll(tail[0:RHS], 3, axis=0), 0.0))
        weights[F:ROWS, part] = jnp.concatenate([swapped, jnp.zeros_like(swapped)], axis=0).astype(BF16)

    acc[...] = jnp.zeros_like(acc)

    def first_pass(t, carry):
        g = (x + t) % nx
        slots = jbuf.at[pl.ds(g * ny, ny)]
        wait_bytes(slots, r_row.at[g])
        block = jnp.concatenate([jbuf[g * ny + k] for k in range(ny)], axis=1)
        inner = lax.dot_general(block, weights[...], (((0,), (0,)), ((), ())), preferred_element_type=F32)
        kern = jnp.exp(inner).astype(BF16)
        tile[pl.ds(pl.multiple_of(g * group, group), group), :] = kern
        acc[...] += jnp.dot(block[F:ROWS], kern, preferred_element_type=F32)
        return carry

    lax.fori_loop(0, nx, first_pass, 0)

    to_cols(lambda peer: acc.at[pl.ds(RHS, RHS), pl.ds(pl.multiple_of(peer * LANES, LANES), LANES)],
            rs1.at[col], s_rs1, r_rs1)
    scale = amp[...]
    shift = noise[...]
    wait_bytes(rs1, r_rs1)
    q1 = scale * jnp.sum(rs1[...], axis=0) + shift * low
    msg2[0:RHS, :] = q1
    msg2[RHS:2 * RHS, :] = jnp.where(
        lane == 0, jnp.sum(v0 * v0, axis=1, keepdims=True),
        jnp.where(lane == 1, jnp.sum(low * q1, axis=1, keepdims=True), 0.0))
    to_rows(msg2, j2.at[row], s_row2, r_row2.at[x])
    to_cols(lambda peer: msg2, i2.at[col], s_col2, r_col2)

    wait_bytes(rs1.at[pl.ds(0, nc - 1)], s_rs1)
    acc[...] = jnp.zeros_like(acc)

    def second_pass(t, total):
        g = (x + t) % nx
        wait_bytes(j2.at[pl.ds(g * ny, ny)], r_row2.at[g])
        parts = [j2[g * ny + k] for k in range(ny)]
        for part in parts:
            total = total + part[RHS:2 * RHS]
        value = jnp.concatenate([part[0:RHS] for part in parts], axis=1)
        high = value.astype(BF16).astype(F32)
        both = jnp.concatenate([high, value - high], axis=0).astype(BF16)
        acc[...] += jnp.dot(both, tile[pl.ds(pl.multiple_of(g * group, group), group), :],
                            preferred_element_type=F32)
        return total

    scal1[...] = lax.fori_loop(0, nx, second_pass, jnp.zeros((RHS, LANES), F32))
    to_cols(lambda peer: scal1, sc1.at[col], s_sc, r_sc)
    wait_bytes(i2, r_col2)
    wait_bytes(sc1, r_sc)
    sums1 = jnp.sum(sc1[...], axis=0)
    rr0 = sums1[:, 0:1]
    curve1 = sums1[:, 1:2]
    alpha1 = rr0 / curve1
    r1 = v0 - alpha1 * q1

    cross = jnp.zeros((RHS, LANES), F32)
    for c in range(nc):
        part = slice(c * LANES, (c + 1) * LANES)
        second = acc[0:RHS, part] + acc[RHS:2 * RHS, part]
        send2[c, 0:RHS, :] = second
        tail = ibuf[c, F:ROWS, :].astype(F32)
        mine = tail[RHS:2 * RHS] + jnp.where(sub == 0, tail[6:7], 0.0)
        cross = cross + (mine - alpha1 * i2[c, 0:RHS, :]) * second
    cross = scale * cross + shift * r1 * q1
    sums = jnp.where(
        lane == 0, jnp.sum(cross, axis=1, keepdims=True), jnp.where(
            lane == 1, jnp.sum(r1 * r1, axis=1, keepdims=True), jnp.where(
                lane == 2, jnp.sum(r1 * q1, axis=1, keepdims=True), 0.0)))
    for c in range(nc):
        send2[c, RHS:2 * RHS, :] = sums
    to_cols(lambda peer: send2.at[peer], rs2.at[col], s_rs2, r_rs2)
    wait_bytes(rs2, r_rs2)
    fin_msg[...] = jnp.sum(rs2[:, RHS:2 * RHS, :], axis=0)
    to_rows(fin_msg, fin.at[row], s_fin, r_fin)
    q2 = scale * jnp.sum(rs2[:, 0:RHS, :], axis=0) + shift * q1
    wait_bytes(fin, r_fin)
    sums2 = jnp.sum(fin[...], axis=0)
    r1q2, rr1, r1q1 = sums2[:, 0:1], sums2[:, 1:2], sums2[:, 2:3]
    beta = rr1 / rr0
    curve2 = (r1q1 - alpha1 * r1q2) + 2.0 * beta * r1q1 + beta * beta * curve1
    alpha2 = rr1 / curve2
    d2 = r1 + beta * v0
    image2 = (q1 - alpha1 * q2) + beta * q1
    sol[...] = alpha1 * v0 + alpha2 * d2
    res[...] = r1 - alpha2 * image2

    wait_bytes(ibuf.at[pl.ds(0, nc - 1)], s_col)
    wait_bytes(jbuf.at[pl.ds(0, nr - 1)], s_row)
    wait_bytes(j2.at[pl.ds(0, nr - 1)], s_row2)
    wait_bytes(i2.at[pl.ds(0, nc - 1)], s_col2)
    wait_bytes(sc1.at[pl.ds(0, nc - 1)], s_sc)
    wait_bytes(rs2.at[pl.ds(0, nc - 1)], s_rs2)
    wait_bytes(fin.at[pl.ds(0, nr - 1)], s_fin)


def solution(mesh):
    nr, nc = mesh.shape["row"], mesh.shape["col"]
    ny = 8 if nr % 8 == 0 else nr
    nx = nr // ny
    vmem = pl.BlockSpec(memory_space=pltpu.VMEM)
    dma = pltpu.SemaphoreType.DMA

    def shards(points, inv_scale, amplitude, noise, targets, probe_seeds):
        out = jax.ShapeDtypeStruct((RHS, LANES), F32)
        return pl.pallas_call(
            lambda *refs: body(nx, ny, nc, refs),
            out_shape=(out, out),
            in_specs=[vmem] * 6,
            out_specs=(vmem, vmem),
            scratch_shapes=[
                pltpu.VMEM((ROWS, LANES), BF16),
                pltpu.VMEM((nr, ROWS, LANES), BF16),
                pltpu.VMEM((nc, ROWS, LANES), BF16),
                pltpu.VMEM((ROWS, nc * LANES), BF16),
                pltpu.VMEM((nr * LANES, nc * LANES), BF16),
                pltpu.VMEM((2 * RHS, nc * LANES), F32),
                pltpu.VMEM((nc, RHS, LANES), F32),
                pltpu.VMEM((2 * RHS, LANES), F32),
                pltpu.VMEM((nr, 2 * RHS, LANES), F32),
                pltpu.VMEM((nc, 2 * RHS, LANES), F32),
                pltpu.VMEM((nc, RHS, LANES), F32),
                pltpu.VMEM((RHS, LANES), F32),
                pltpu.VMEM((nc, 2 * RHS, LANES), F32),
                pltpu.VMEM((nc, 2 * RHS, LANES), F32),
                pltpu.VMEM((RHS, LANES), F32),
                pltpu.VMEM((nr, RHS, LANES), F32),
                dma, dma, dma((nx,)), dma, dma, dma, dma, dma, dma((nx,)), dma,
                dma, dma, dma, dma, dma, dma,
            ],
            compiler_params=pltpu.CompilerParams(
                collective_id=0, has_side_effects=True, vmem_limit_bytes=48 * 2**20),
        )(points, inv_scale.reshape(1, F), amplitude.reshape(1, 1), noise.reshape(1, LANES),
          targets.reshape(1, LANES), probe_seeds.reshape(1, LANES))

    spec = P(("row", "col"))
    both = P(None, ("row", "col"))
    return jax.shard_map(
        shards, mesh=mesh, in_specs=(both, P(), P(), spec, spec, spec),
        out_specs=(both, both), check_vma=False)
```

time: 684 us -> 73.3 us (0.11)
  blocking collectives: 349 us -> 0 us
  waiting for transfers between devices: 209 us -> 0 us
  starting transfers between devices: 81.5 us -> 0 us
  Pallas kernels: 0 us -> 69.9 us
  matrix products: 15.1 us -> 0 us
  between operations: 15.3 us -> 1.35 us
  other arithmetic: 11 us -> 0 us
    psum x3 -> x0, blocking collectives: 294 us -> none  [the longest x2 194 us: squares(): return lax.psum(jnp.sum(residual * residual, axis=1), ('row', 'col'))]
    reduce_scatter x2 -> x0, waiting for transfers between devices: 120 us -> none  [shards(): lax.psum_scatter(forward + arrived, 'col', scatter_dimension=1, tiled=True)]
    ppermute x25 -> x0, waiting for transfers between devices: 89.2 us -> none  [shifted(): return lax.ppermute(value, axis, pairs)]
    ppermute x25 -> x0, starting transfers between devices: 81.5 us -> none  [shifted(): return lax.ppermute(value, axis, pairs)]
    pallas_call x0 -> x1, Pallas kernels: none -> 69.9 us  [shards(): pl.pallas_call(lambda *refs: body(nx, ny, nc, refs), out_shape=(out, out)...]
    all_gather x3 -> x0, blocking collectives: 55.5 us -> none  [the longest x2 40.7 us: shards(): block_dirs = lax.all_gather(low, 'col', axis=1, tiled=True)]
    dot_general x24 -> x0, matrix products: 15.1 us -> none  [the longest x8 6.81 us: kernel_tile(): lax.dot_general(row_points, col_points, (((0,), (0,)), ((), ())), preferr...]
  transfers between devices with their start and end apart: 27 -> 0, of which waited for: 20 -> 0; matrix products, arithmetic and copies ran while one was open for 0% -> 0% of each run, Pallas kernels for 0% -> 0%
where the time goes in v1:
time: 73.3 us; the launch traced here: 73.1 us
  Pallas kernels  69.9 us (95%)
  local copies, waits for them, and re-layouts  1.85 us (3%)
  between operations  1.35 us (2%)
    pallas_call x1, Pallas kernels, shards(): pl.pallas_call(lambda *refs: body(nx, ny, nc, refs), out_shape=(out, out)...  69.9 us
    unnamed x12, local copies, waits for them, and re-layouts  1.85 us

profile of v1, /device:TPU:1, one launch (start us, length us, event | category | flops | bytes accessed | tf_op | source)
XLA Modules:
  0.0 73.1 jit_solution(5249146486391236289)
XLA Ops:
  0.6 0.0 copy-start
  1.3 0.0 copy-start.4
  1.3 0.0 copy-start.1
  1.3 0.0 copy-start.2
  1.3 0.0 copy-start.3
  1.3 0.0 copy-done
  1.3 0.6 copy-done.4
  2.0 0.0 copy-done.1
  2.0 0.0 copy-done.2
  2.0 0.0 copy-done.3
  2.0 69.9 %shard_map.77 = (f32[8,128]{1,0:T(8,128)S(1)}, f32[8,128]{1,0:T(8,128)S(1)}) custom-call(bf16[32,128]{1,0:T(8,128)(2,1)S(1)} %copy-done, f32[1,32]{1,0:T(1,128)S(1)} %bitcast.6, f32[1,1]{1,0:T(1,128)} %bitcast.5.refs_2_, f32[1,128]{1,0:T(1,128)S(1)} %bitcast.7, f32[1,128]{1,0:T(1,128)S(1)} %bitcast.8, s32[1,128]{1,0:T(1,128)S(1)} %bitcast.9), custom_call_target="tpu_custom_call" | custom-call | tf_op jit(solution)/shard_map/pallas_call | solution.py:219
  71.9 0.6 copy.11
  72.5 0.6 copy.12
Async XLA Ops:
  0.6 0.7 copy-start
  1.3 0.7 copy-start.4
  1.3 0.7 copy-start.1
  1.3 0.7 copy-start.2
  1.3 0.7 copy-start.3

commit v2 on v1

v2 whole, which is shorter than its diff:
```python
import jax
import jax.numpy as jnp
from jax import lax
from jax.experimental import pallas as pl
from jax.experimental.pallas import tpu as pltpu
from jax.sharding import PartitionSpec as P

MESH = pl.DeviceIdType.MESH
F = 32
TAIL = 16
ROWS = F + TAIL
RHS = 8
LANES = 128
F32 = jnp.float32
BF16 = jnp.bfloat16


def pieces(value):
    first = value.astype(BF16).astype(F32)
    rest = value - first
    second = rest.astype(BF16).astype(F32)
    return first, second, rest - second


def wait_bytes(ref, sem):
    pltpu.make_async_copy(ref, ref, sem).wait()


def body(nx, ny, nc, refs):
    (points_in, inv_in, amp_in, noise_in, targets_in, seeds_in, sol, res) = refs[:8]
    (points, inv, amp, noise, targets, seeds) = refs[8:14]
    (pts, aux, jp, ja, ip, ia, weights, v_i, tile, acc, rs1, s1_msg, s1_col, s1_sum, s1_row,
     q1_msg, j2, i2, out2, s2_msg, s2_col, rs2, s2_sum, s2_row) = refs[14:38]
    (in_sem, s_pc, s_pr, r_pc, r_pr, s_ac, s_ar, r_ac, r_ar, s_rs1, r_rs1, s_s1c, r_s1c, s_s1r, r_s1r,
     s_q1c, s_q1r, r_q1c, r_q1r, s_s2c, r_s2c, s_rs2, r_rs2, s_s2r, r_s2r) = refs[38:]
    nr = nx * ny
    group = ny * LANES
    row = lax.axis_index("row")
    col = lax.axis_index("col")
    x = row // ny
    y = row % ny

    def turn(t):
        return (t * (7 - t) // 2) % 4 if nx == 4 else t

    def row_peer(k):
        return ((x + nx - turn(k // ny)) % nx) * ny + (y + k % ny) % ny

    def col_peer(k):
        return (col + k) % nc

    def to_rows(*copies):
        for src, dst, send, recv in copies:
            pltpu.make_async_copy(src, dst, recv).start()

        def go(k, carry):
            peer = row_peer(k)
            for src, dst, send, recv in copies:
                pltpu.make_async_remote_copy(
                    src_ref=src, dst_ref=dst, send_sem=send, recv_sem=recv,
                    device_id=(peer, col), device_id_type=MESH,
                ).start()
            return carry

        lax.fori_loop(1, nr, go, 0)

    def to_cols(*copies):
        for src_of, dst, send, recv in copies:
            pltpu.make_async_copy(src_of(col), dst, recv).start()

        def go(k, carry):
            peer = col_peer(k)
            for src_of, dst, send, recv in copies:
                pltpu.make_async_remote_copy(
                    src_ref=src_of(peer), dst_ref=dst, send_sem=send, recv_sem=recv,
                    device_id=(row, peer), device_id_type=MESH,
                ).start()
            return carry

        lax.fori_loop(1, nc, go, 0)

    loads = [pltpu.make_async_copy(a, b, in_sem.at[n]) for n, (a, b) in enumerate((
        (points_in, points), (inv_in, inv), (targets_in, targets), (seeds_in, seeds),
        (noise_in, noise), (amp_in, amp)))]
    for load in loads:
        load.start()

    barrier = pltpu.get_barrier_semaphore()

    def greet_row(k, carry):
        pl.semaphore_signal(barrier, inc=1, device_id=(row_peer(k), col), device_id_type=MESH)
        return carry

    def greet_col(k, carry):
        pl.semaphore_signal(barrier, inc=1, device_id=(row, col_peer(k)), device_id_type=MESH)
        return carry

    lax.fori_loop(1, nr, greet_row, 0)
    lax.fori_loop(1, nc, greet_col, 0)

    sub = lax.broadcasted_iota(jnp.int32, (RHS, LANES), 0)
    lane = lax.broadcasted_iota(jnp.int32, (RHS, LANES), 1)

    def build_rhs(target, seed):
        bits = (seed.astype(jnp.int32) >> jnp.maximum(sub - 1, 0)) & 1
        return jnp.where(sub == 0, target, (1 - 2 * bits).astype(F32))

    def minus_half_norm(block):
        values = block.astype(F32)
        return -0.5 * jnp.sum(values * values, axis=0, keepdims=True)

    def as_row(sums):
        spread = jnp.zeros((RHS, LANES), F32)
        for q, value in enumerate(sums):
            spread = spread + jnp.where(lane == q * RHS + sub, value, 0.0)
        return jnp.sum(spread, axis=0, keepdims=True)

    def from_row(total, q):
        return jnp.sum(jnp.where(lane == q * RHS + sub, total, 0.0), axis=1, keepdims=True)

    def rowsum(value):
        return jnp.sum(value, axis=1, keepdims=True)

    for load in loads:
        load.wait()
    eye = lax.broadcasted_iota(jnp.int32, (F, F), 0) == lax.broadcasted_iota(jnp.int32, (F, F), 1)
    factor = jnp.sum(jnp.where(eye, inv[...], 0.0), axis=1, keepdims=True)
    pts[...] = (points[...].astype(F32) * factor).astype(BF16)
    aux[0:1, :] = targets[...]
    aux[1:2, :] = seeds[...].astype(F32)

    pl.semaphore_wait(barrier, nr - 1 + nc - 1)
    to_cols((lambda peer: aux, ia.at[col], s_ac, r_ac), (lambda peer: pts, ip.at[col], s_pc, r_pc))
    to_rows((aux, ja.at[row], s_ar, r_ar.at[x]), (pts, jp.at[row], s_pr, r_pr.at[x]))
    v0 = build_rhs(targets[...], seeds[...])
    low = v0.astype(BF16).astype(F32)
    scale = amp[...]
    shift = noise[...]
    acc[...] = jnp.zeros_like(acc)

    wait_bytes(ia, r_ac)
    wait_bytes(ip, r_pc)
    for c in range(nc):
        part = slice(c * LANES, (c + 1) * LANES)
        block = ip[c]
        n1, n2, n3 = pieces(minus_half_norm(block))
        weights[0:F, part] = block
        extra = jnp.where(sub < 3, 1.0, jnp.where(sub == 3, n1, jnp.where(sub == 4, n2, jnp.where(sub == 5, n3, 0.0))))
        weights[F:ROWS, part] = jnp.concatenate([extra, jnp.zeros_like(extra)], axis=0).astype(BF16)
        v_i[:, part] = build_rhs(ia[c, 0:1], ia[c, 1:2])

    def first_pass(t, carry):
        g = (x + turn(t)) % nx
        wait_bytes(ja.at[pl.ds(g * ny, ny)], r_ar.at[g])
        wait_bytes(jp.at[pl.ds(g * ny, ny)], r_pr.at[g])
        blocks, tails = [], []
        for k in range(ny):
            block = jp[g * ny + k]
            info = ja[g * ny + k]
            n1, n2, n3 = pieces(minus_half_norm(block))
            extra = jnp.where(sub == 0, n1, jnp.where(sub == 1, n2, jnp.where(sub == 2, n3, jnp.where(sub < 6, 1.0, 0.0))))
            blocks.append(block)
            tails.append(jnp.concatenate([extra, build_rhs(info[0:1], info[1:2])], axis=0).astype(BF16))
        tail = jnp.concatenate(tails, axis=1)
        block = jnp.concatenate([jnp.concatenate(blocks, axis=1), tail], axis=0)
        inner = lax.dot_general(block, weights[...], (((0,), (0,)), ((), ())), preferred_element_type=F32)
        kern = jnp.exp(inner).astype(BF16)
        tile[pl.ds(pl.multiple_of(g * group, group), group), :] = kern
        acc[...] += jnp.dot(tail, kern, preferred_element_type=F32)
        return carry

    lax.fori_loop(0, nx, first_pass, 0)

    to_cols((lambda peer: acc.at[pl.ds(RHS, RHS), pl.ds(pl.multiple_of(peer * LANES, LANES), LANES)],
             rs1.at[col], s_rs1, r_rs1))
    low_i = v_i[...].astype(BF16).astype(F32)
    s1_msg[...] = as_row((
        rowsum(v0 * v0), scale * rowsum(low_i * acc[RHS:2 * RHS, :]) + rowsum(shift * low * low)))
    to_cols((lambda peer: s1_msg, s1_col.at[col], s_s1c, r_s1c))
    wait_bytes(rs1, r_rs1)
    q1 = scale * jnp.sum(rs1[...], axis=0) + shift * low
    q1_msg[...] = q1
    to_rows((q1_msg, j2.at[row], s_q1r, r_q1r.at[x]))
    to_cols((lambda peer: q1_msg, i2.at[col], s_q1c, r_q1c))
    wait_bytes(s1_col, r_s1c)
    s1_sum[...] = jnp.sum(s1_col[...], axis=0)
    to_rows((s1_sum, s1_row.at[row], s_s1r, r_s1r))

    wait_bytes(rs1.at[pl.ds(0, nc - 1)], s_rs1)
    acc[...] = jnp.zeros_like(acc)

    def second_pass(t, carry):
        g = (x + turn(t)) % nx
        wait_bytes(j2.at[pl.ds(g * ny, ny)], r_q1r.at[g])
        value = jnp.concatenate([j2[g * ny + k] for k in range(ny)], axis=1)
        high = value.astype(BF16).astype(F32)
        both = jnp.concatenate([high, value - high], axis=0).astype(BF16)
        acc[...] += jnp.dot(both, tile[pl.ds(pl.multiple_of(g * group, group), group), :],
                            preferred_element_type=F32)
        return carry

    lax.fori_loop(0, nx, second_pass, 0)
    wait_bytes(i2, r_q1c)
    wait_bytes(s1_row, r_s1r)
    total1 = jnp.sum(s1_row[...], axis=0)
    rr0 = from_row(total1, 0)
    curve1 = from_row(total1, 1)
    alpha1 = rr0 / curve1
    r1 = v0 - alpha1 * q1

    cross = jnp.zeros((RHS, LANES), F32)
    for c in range(nc):
        part = slice(c * LANES, (c + 1) * LANES)
        second = acc[0:RHS, part] + acc[RHS:2 * RHS, part]
        out2[c] = second
        cross = cross + (v_i[:, part] - alpha1 * i2[c]) * second
    s2_msg[...] = as_row((rowsum(scale * cross + shift * r1 * q1), rowsum(r1 * r1), rowsum(r1 * q1)))
    to_cols((lambda peer: s2_msg, s2_col.at[col], s_s2c, r_s2c))
    to_cols((lambda peer: out2.at[peer], rs2.at[col], s_rs2, r_rs2))
    wait_bytes(s2_col, r_s2c)
    s2_sum[...] = jnp.sum(s2_col[...], axis=0)
    to_rows((s2_sum, s2_row.at[row], s_s2r, r_s2r))
    wait_bytes(rs2, r_rs2)
    q2 = scale * jnp.sum(rs2[...], axis=0) + shift * q1

    wait_bytes(ip.at[pl.ds(0, nc - 1)], s_pc)
    wait_bytes(jp.at[pl.ds(0, nr - 1)], s_pr)
    wait_bytes(ia.at[pl.ds(0, nc - 1)], s_ac)
    wait_bytes(ja.at[pl.ds(0, nr - 1)], s_ar)
    wait_bytes(s1_col.at[pl.ds(0, nc - 1)], s_s1c)
    wait_bytes(s1_row.at[pl.ds(0, nr - 1)], s_s1r)
    wait_bytes(j2.at[pl.ds(0, nr - 1)], s_q1r)
    wait_bytes(i2.at[pl.ds(0, nc - 1)], s_q1c)
    wait_bytes(s2_col.at[pl.ds(0, nc - 1)], s_s2c)
    wait_bytes(rs2.at[pl.ds(0, nc - 1)], s_rs2)
    wait_bytes(s2_row.at[pl.ds(0, nr - 1)], s_s2r)

    wait_bytes(s2_row, r_s2r)
    total2 = jnp.sum(s2_row[...], axis=0)
    r1q2, rr1, r1q1 = (from_row(total2, q) for q in range(3))
    beta = rr1 / rr0
    curve2 = (r1q1 - alpha1 * r1q2) + 2.0 * beta * r1q1 + beta * beta * curve1
    alpha2 = rr1 / curve2
    d2 = r1 + beta * v0
    image2 = (q1 - alpha1 * q2) + beta * q1
    sol[...] = alpha1 * v0 + alpha2 * d2
    res[...] = r1 - alpha2 * image2


def solution(mesh):
    nr, nc = mesh.shape["row"], mesh.shape["col"]
    ny = 8 if nr % 8 == 0 else nr
    nx = nr // ny
    vmem = pl.BlockSpec(memory_space=pltpu.VMEM)
    anywhere = pl.BlockSpec(memory_space=pl.ANY)
    dma = pltpu.SemaphoreType.DMA

    def shards(points, inv_scale, amplitude, noise, targets, probe_seeds):
        out = jax.ShapeDtypeStruct((RHS, LANES), F32)
        line = pltpu.VMEM((1, LANES), F32)
        plane = pltpu.VMEM((RHS, LANES), F32)
        return pl.pallas_call(
            lambda *refs: body(nx, ny, nc, refs),
            out_shape=(out, out),
            in_specs=[anywhere] * 6,
            out_specs=(vmem, vmem),
            scratch_shapes=[
                pltpu.VMEM((F, LANES), BF16), pltpu.VMEM((1, F), F32), pltpu.VMEM((1, 1), F32),
                line, line, pltpu.VMEM((1, LANES), jnp.int32),
                pltpu.VMEM((F, LANES), BF16), pltpu.VMEM((2, LANES), F32),
                pltpu.VMEM((nr, F, LANES), BF16), pltpu.VMEM((nr, 2, LANES), F32),
                pltpu.VMEM((nc, F, LANES), BF16), pltpu.VMEM((nc, 2, LANES), F32),
                pltpu.VMEM((ROWS, nc * LANES), BF16), pltpu.VMEM((RHS, nc * LANES), F32),
                pltpu.VMEM((nr * LANES, nc * LANES), BF16), pltpu.VMEM((2 * RHS, nc * LANES), F32),
                pltpu.VMEM((nc, RHS, LANES), F32), line, pltpu.VMEM((nc, 1, LANES), F32), line,
                pltpu.VMEM((nr, 1, LANES), F32),
                plane, pltpu.VMEM((nr, RHS, LANES), F32), pltpu.VMEM((nc, RHS, LANES), F32),
                pltpu.VMEM((nc, RHS, LANES), F32),
                line, pltpu.VMEM((nc, 1, LANES), F32), pltpu.VMEM((nc, RHS, LANES), F32), line,
                pltpu.VMEM((nr, 1, LANES), F32),
                dma((6,)), dma, dma, dma, dma((nx,)), dma, dma, dma, dma((nx,)), dma, dma, dma, dma, dma, dma,
                dma, dma, dma, dma((nx,)), dma, dma, dma, dma, dma, dma,
            ],
            compiler_params=pltpu.CompilerParams(
                collective_id=0, has_side_effects=True, vmem_limit_bytes=48 * 2**20),
        )(points, inv_scale.reshape(1, F), amplitude.reshape(1, 1), noise.reshape(1, LANES),
          targets.reshape(1, LANES), probe_seeds.reshape(1, LANES))

    spec = P(("row", "col"))
    both = P(None, ("row", "col"))
    return jax.shard_map(
        shards, mesh=mesh, in_specs=(both, P(), P(), spec, spec, spec),
        out_specs=(both, both), check_vma=False)
```

time: 73.3 us -> 59.4 us (0.81)
  Pallas kernels: 69.9 us -> 56 us
    pallas_call x1, Pallas kernels: 69.9 us -> 56 us  [shards(): pl.pallas_call(lambda *refs: body(nx, ny, nc, refs), out_shape=(out, out)...]
where the time goes in v2:
time: 59.4 us; the launch traced here: 59.2 us
  Pallas kernels  56 us (94%)
  local copies, waits for them, and re-layouts  1.85 us (3%)
  between operations  1.35 us (2%)
    pallas_call x1, Pallas kernels, shards(): pl.pallas_call(lambda *refs: body(nx, ny, nc, refs), out_shape=(out, out)...  56 us
    unnamed x12, local copies, waits for them, and re-layouts  1.85 us

profile of v2, /device:TPU:1, one launch (start us, length us, event | category | flops | bytes accessed | tf_op | source)
XLA Modules:
  0.0 59.2 jit_solution(9317375188298756059)
XLA Ops:
  0.6 0.0 copy-start
  1.3 0.0 copy-start.4
  1.3 0.0 copy-start.1
  1.3 0.0 copy-start.2
  1.3 0.0 copy-start.3
  1.3 0.0 copy-done
  1.3 0.6 %copy-done.4 = s32[128]{0:T(128)S(1)} copy-done((s32[128]{0:T(128)S(1)}, s32[128]{0:T(128)}, u32[]{:S(2)}) %copy-start.4) | copy-done | bytes 536
  2.0 0.0 copy-done.1
  2.0 0.0 copy-done.2
  2.0 0.0 copy-done.3
  2.0 56.0 %shard_map.77 = (f32[8,128]{1,0:T(8,128)S(1)}, f32[8,128]{1,0:T(8,128)S(1)}) custom-call(bf16[32,128]{1,0:T(8,128)(2,1)S(1)} %copy-done, f32[1,32]{1,0:T(1,128)S(1)} %bitcast.6, f32[1,1]{1,0:T(1,128)} %bitcast.5.refs_2_, f32[1,128]{1,0:T(1,128)S(1)} %bitcast.7, f32[1,128]{1,0:T(1,128)S(1)} %bitcast.8, s32[1,128]{1,0:T(1,128)S(1)} %bitcast.9), custom_call_target="tpu_custom_call" | custom-call | tf_op jit(solution)/shard_map/pallas_call | solution.py:262
  58.0 0.6 %copy.11 = f32[8,128]{1,0:T(8,128)} copy(f32[8,128]{1,0:T(8,128)S(1)} %get-tuple-element.4) | data formatting | bytes 8192
  58.6 0.6 copy.12
Async XLA Ops:
  0.6 0.7 %copy-start = (bf16[32,128]{1,0:T(8,128)(2,1)S(1)}, bf16[32,128]{1,0:T(8,128)(2,1)}, u32[]{:S(2)}) copy-start(bf16[32,128]{1,0:T(8,128)(2,1)} %refs_0_.1) | copy-start | bytes 24580
  1.3 0.7 %copy-start.4 = (s32[128]{0:T(128)S(1)}, s32[128]{0:T(128)}, u32[]{:S(2)}) copy-start(s32[128]{0:T(128)} %param.11) | copy-start | bytes 1540
  1.3 0.7 %copy-start.1 = (f32[32]{0:T(128)S(1)}, f32[32]{0:T(128)}, u32[]{:S(2)}) copy-start(f32[32]{0:T(128)} %param.7) | copy-start | bytes 388
  1.3 0.7 %copy-start.2 = (f32[128]{0:T(128)S(1)}, f32[128]{0:T(128)}, u32[]{:S(2)}) copy-start(f32[128]{0:T(128)} %param.9) | copy-start | bytes 1540
  1.3 0.7 %copy-start.3 = (f32[128]{0:T(128)S(1)}, f32[128]{0:T(128)}, u32[]{:S(2)}) copy-start(f32[128]{0:T(128)} %param.10) | copy-start | bytes 1540

commit v3 on v2

--- a/solution.py
+++ b/solution.py
@@ -31,7 +31,7 @@
     (points, inv, amp, noise, targets, seeds) = refs[8:14]
     (pts, aux, jp, ja, ip, ia, weights, v_i, tile, acc, rs1, s1_msg, s1_col, s1_sum, s1_row,
      q1_msg, j2, i2, out2, s2_msg, s2_col, rs2, s2_sum, s2_row) = refs[14:38]
-    (in_sem, s_pc, s_pr, r_pc, r_pr, s_ac, s_ar, r_ac, r_ar, s_rs1, r_rs1, s_s1c, r_s1c, s_s1r, r_s1r,
+    (in_sem, s_pc, s_pr, s_px, r_pc, r_py, r_px, s_ac, s_ar, s_ax, r_ac, r_ay, r_ax, s_rs1, r_rs1, s_s1c, r_s1c, s_s1r, r_s1r,
      s_q1c, s_q1r, r_q1c, r_q1r, s_s2c, r_s2c, s_rs2, r_rs2, s_s2r, r_s2r) = refs[38:]
     nr = nx * ny
     group = ny * LANES
@@ -48,6 +48,16 @@
 
     def col_peer(k):
         return (col + k) % nc
+
+    def y_peer(k):
+        return (x * ny + (y + k) % ny, col)
+
+    def x_peer(k):
+        return (((x + k) % nx) * ny + y, col)
+
+    def near(t):
+        half = t // 2 + 1
+        return half + (t % 2) * (ny - 2 * half)
 
     def to_rows(*copies):
         for src, dst, send, recv in copies:
@@ -87,16 +97,16 @@
 
     barrier = pltpu.get_barrier_semaphore()
 
-    def greet_row(k, carry):
-        pl.semaphore_signal(barrier, inc=1, device_id=(row_peer(k), col), device_id_type=MESH)
-        return carry
-
-    def greet_col(k, carry):
-        pl.semaphore_signal(barrier, inc=1, device_id=(row, col_peer(k)), device_id_type=MESH)
-        return carry
-
-    lax.fori_loop(1, nr, greet_row, 0)
-    lax.fori_loop(1, nc, greet_col, 0)
+    def greet(peer_of):
+        def go(k, carry):
+            pl.semaphore_signal(barrier, inc=1, device_id=peer_of(k), device_id_type=MESH)
+            return carry
+
+        return go
+
+    lax.fori_loop(1, ny, greet(y_peer), 0)
+    lax.fori_loop(1, nx, greet(x_peer), 0)
+    lax.fori_loop(1, nc, greet(lambda k: (row, col_peer(k))), 0)
 
     sub = lax.broadcasted_iota(jnp.int32, (RHS, LANES), 0)
     lane = lax.broadcasted_iota(jnp.int32, (RHS, LANES), 1)
@@ -129,9 +139,43 @@
     aux[0:1, :] = targets[...]
     aux[1:2, :] = seeds[...].astype(F32)
 
-    pl.semaphore_wait(barrier, nr - 1 + nc - 1)
+    pl.semaphore_wait(barrier, ny - 1 + nx - 1 + nc - 1)
     to_cols((lambda peer: aux, ia.at[col], s_ac, r_ac), (lambda peer: pts, ip.at[col], s_pc, r_pc))
-    to_rows((aux, ja.at[row], s_ar, r_ar.at[x]), (pts, jp.at[row], s_pr, r_pr.at[x]))
+
+    def copy_to(device, src, dst, send, recv):
+        pltpu.make_async_remote_copy(
+            src_ref=src, dst_ref=dst, send_sem=send, recv_sem=recv,
+            device_id=device, device_id_type=MESH,
+        ).start()
+
+    def forward(slot):
+        def go(k, carry):
+            copy_to(x_peer(k), ja.at[slot], ja.at[slot], s_ax, r_ax.at[x])
+            copy_to(x_peer(k), jp.at[slot], jp.at[slot], s_px, r_px.at[x])
+            return carry
+
+        lax.fori_loop(1, nx, go, 0)
+
+    def to_ring(t, carry):
+        peer = y_peer(near(ny - 2 - t))
+        copy_to(peer, aux, ja.at[row], s_ar, r_ay.at[y])
+        copy_to(peer, pts, jp.at[row], s_pr, r_py.at[y])
+        return carry
+
+    lax.fori_loop(0, ny - 1, to_ring, 0)
+    ja[row] = aux[...]
+    jp[row] = pts[...]
+    forward(row)
+
+    def pass_on(t, carry):
+        source = (y + near(t)) % ny
+        slot = x * ny + source
+        wait_bytes(ja.at[slot], r_ay.at[source])
+        wait_bytes(jp.at[slot], r_py.at[source])
+        forward(slot)
+        return carry
+
+    lax.fori_loop(0, ny - 1, pass_on, 0)
     v0 = build_rhs(targets[...], seeds[...])
     low = v0.astype(BF16).astype(F32)
     scale = amp[...]
@@ -151,8 +195,12 @@
 
     def first_pass(t, carry):
         g = (x + turn(t)) % nx
-        wait_bytes(ja.at[pl.ds(g * ny, ny)], r_ar.at[g])
-        wait_bytes(jp.at[pl.ds(g * ny, ny)], r_pr.at[g])
+
+        @pl.when(t > 0)
+        def _():
+            wait_bytes(ja.at[pl.ds(g * ny, ny)], r_ax.at[g])
+            wait_bytes(jp.at[pl.ds(g * ny, ny)], r_px.at[g])
+
         blocks, tails = [], []
         for k in range(ny):
             block = jp[g * ny + k]
@@ -181,10 +229,10 @@
     q1 = scale * jnp.sum(rs1[...], axis=0) + shift * low
     q1_msg[...] = q1
     to_rows((q1_msg, j2.at[row], s_q1r, r_q1r.at[x]))
-    to_cols((lambda peer: q1_msg, i2.at[col], s_q1c, r_q1c))
     wait_bytes(s1_col, r_s1c)
     s1_sum[...] = jnp.sum(s1_col[...], axis=0)
     to_rows((s1_sum, s1_row.at[row], s_s1r, r_s1r))
+    to_cols((lambda peer: q1_msg, i2.at[col], s_q1c, r_q1c))
 
     wait_bytes(rs1.at[pl.ds(0, nc - 1)], s_rs1)
     acc[...] = jnp.zeros_like(acc)
@@ -224,9 +272,11 @@
     q2 = scale * jnp.sum(rs2[...], axis=0) + shift * q1
 
     wait_bytes(ip.at[pl.ds(0, nc - 1)], s_pc)
-    wait_bytes(jp.at[pl.ds(0, nr - 1)], s_pr)
+    wait_bytes(jp.at[pl.ds(0, ny - 1)], s_pr)
+    wait_bytes(jp.at[pl.ds(0, nr - ny)], s_px)
     wait_bytes(ia.at[pl.ds(0, nc - 1)], s_ac)
-    wait_bytes(ja.at[pl.ds(0, nr - 1)], s_ar)
+    wait_bytes(ja.at[pl.ds(0, ny - 1)], s_ar)
+    wait_bytes(ja.at[pl.ds(0, nr - ny)], s_ax)
     wait_bytes(s1_col.at[pl.ds(0, nc - 1)], s_s1c)
     wait_bytes(s1_row.at[pl.ds(0, nr - 1)], s_s1r)
     wait_bytes(j2.at[pl.ds(0, nr - 1)], s_q1r)
@@ -278,7 +328,7 @@
                 pltpu.VMEM((nc, RHS, LANES), F32),
                 line, pltpu.VMEM((nc, 1, LANES), F32), pltpu.VMEM((nc, RHS, LANES), F32), line,
                 pltpu.VMEM((nr, 1, LANES), F32),
-                dma((6,)), dma, dma, dma, dma((nx,)), dma, dma, dma, dma((nx,)), dma, dma, dma, dma, dma, dma,
+                dma((6,)), dma, dma, dma, dma, dma((ny,)), dma((nx,)), dma, dma, dma, dma, dma((ny,)), dma((nx,)), dma, dma, dma, dma, dma, dma,
                 dma, dma, dma, dma((nx,)), dma, dma, dma, dma, dma, dma,
             ],
             compiler_params=pltpu.CompilerParams(

time: 59.4 us -> 57.6 us (0.970)
  Pallas kernels: 56 us -> 54.3 us
    pallas_call x1, Pallas kernels: 56 us -> 54.3 us  [shards(): pl.pallas_call(lambda *refs: body(nx, ny, nc, refs), out_shape=(out, out)...]
where the time goes in v3:
time: 57.6 us; the launch traced here: 57.5 us
  Pallas kernels  54.3 us (94%)
  local copies, waits for them, and re-layouts  1.85 us (3%)
  between operations  1.35 us (2%)
    pallas_call x1, Pallas kernels, shards(): pl.pallas_call(lambda *refs: body(nx, ny, nc, refs), out_shape=(out, out)...  54.3 us
    unnamed x12, local copies, waits for them, and re-layouts  1.85 us

profile of v3, /device:TPU:1, one launch (start us, length us, event | category | flops | bytes accessed | tf_op | source)
XLA Modules:
  0.0 57.5 jit_solution(4871310711438766909)
XLA Ops:
  0.6 0.0 copy-start
  1.3 0.0 copy-start.4
  1.3 0.0 copy-start.1
  1.3 0.0 copy-start.2
  1.3 0.0 copy-start.3
  1.3 0.0 copy-done
  1.3 0.6 %copy-done.4 = s32[128]{0:T(128)S(1)} copy-done((s32[128]{0:T(128)S(1)}, s32[128]{0:T(128)}, u32[]{:S(2)}) %copy-start.4) | copy-done | bytes 536
  2.0 0.0 copy-done.1
  2.0 0.0 copy-done.2
  2.0 0.0 copy-done.3
  2.0 54.3 %shard_map.77 = (f32[8,128]{1,0:T(8,128)S(1)}, f32[8,128]{1,0:T(8,128)S(1)}) custom-call(bf16[32,128]{1,0:T(8,128)(2,1)S(1)} %copy-done, f32[1,32]{1,0:T(1,128)S(1)} %bitcast.6, f32[1,1]{1,0:T(1,128)} %bitcast.5.refs_2_, f32[1,128]{1,0:T(1,128)S(1)} %bitcast.7, f32[1,128]{1,0:T(1,128)S(1)} %bitcast.8, s32[1,128]{1,0:T(1,128)S(1)} %bitcast.9), custom_call_target="tpu_custom_call" | custom-call | tf_op jit(solution)/shard_map/pallas_call | solution.py:312
  56.3 0.6 %copy.11 = f32[8,128]{1,0:T(8,128)} copy(f32[8,128]{1,0:T(8,128)S(1)} %get-tuple-element.4) | data formatting | bytes 8192
  56.9 0.6 %copy.12 = f32[8,128]{1,0:T(8,128)} copy(f32[8,128]{1,0:T(8,128)S(1)} %get-tuple-element.5) | data formatting | bytes 8192
Async XLA Ops:
  0.6 0.7 %copy-start = (bf16[32,128]{1,0:T(8,128)(2,1)S(1)}, bf16[32,128]{1,0:T(8,128)(2,1)}, u32[]{:S(2)}) copy-start(bf16[32,128]{1,0:T(8,128)(2,1)} %refs_0_.1) | copy-start | bytes 24580
  1.3 0.7 %copy-start.4 = (s32[128]{0:T(128)S(1)}, s32[128]{0:T(128)}, u32[]{:S(2)}) copy-start(s32[128]{0:T(128)} %param.11) | copy-start | bytes 1540
  1.3 0.7 %copy-start.1 = (f32[32]{0:T(128)S(1)}, f32[32]{0:T(128)}, u32[]{:S(2)}) copy-start(f32[32]{0:T(128)} %param.7) | copy-start | bytes 388
  1.3 0.7 %copy-start.2 = (f32[128]{0:T(128)S(1)}, f32[128]{0:T(128)}, u32[]{:S(2)}) copy-start(f32[128]{0:T(128)} %param.9) | copy-start | bytes 1540
  1.3 0.7 %copy-start.3 = (f32[128]{0:T(128)S(1)}, f32[128]{0:T(128)}, u32[]{:S(2)}) copy-start(f32[128]{0:T(128)} %param.10) | copy-start | bytes 1540

commit v4 on v3

--- a/solution.py
+++ b/solution.py
@@ -27,27 +27,36 @@
 
 
 def body(nx, ny, nc, refs):
-    (points_in, inv_in, amp_in, noise_in, targets_in, seeds_in, sol, res) = refs[:8]
-    (points, inv, amp, noise, targets, seeds) = refs[8:14]
+    (points_in, inv_in, amp_in, noise_in, targets_in, seeds_in, both) = refs[:7]
+    (points, inv, amp, noise, targets, seeds) = refs[7:13]
     (pts, aux, jp, ja, ip, ia, weights, v_i, tile, acc, rs1, s1_msg, s1_col, s1_sum, s1_row,
-     q1_msg, j2, i2, out2, s2_msg, s2_col, rs2, s2_sum, s2_row) = refs[14:38]
+     q1_msg, j2, i2, out2, s2_msg, s2_col, rs2, s2_sum, s2_row) = refs[13:37]
     (in_sem, s_pc, s_pr, s_px, r_pc, r_py, r_px, s_ac, s_ar, s_ax, r_ac, r_ay, r_ax, s_rs1, r_rs1, s_s1c, r_s1c, s_s1r, r_s1r,
-     s_q1c, s_q1r, r_q1c, r_q1r, s_s2c, r_s2c, s_rs2, r_rs2, s_s2r, r_s2r) = refs[38:]
+     s_q1c, s_q1r, r_q1c, r_q1r, s_s2c, r_s2c, s_rs2, r_rs2, s_s2r, r_s2r) = refs[37:]
     nr = nx * ny
     group = ny * LANES
     row = lax.axis_index("row")
     col = lax.axis_index("col")
     x = row // ny
     y = row % ny
+    nz = nc // 2
+    z = col // 2
+    core = col % 2
 
     def turn(t):
         return (t * (7 - t) // 2) % 4 if nx == 4 else t
 
+    def offset(t, n):
+        half = (t + 1) // 2
+        return (t % 2) * half + (1 - t % 2) * ((n - half) % n)
+
     def row_peer(k):
-        return ((x + nx - turn(k // ny)) % nx) * ny + (y + k % ny) % ny
+        far_y, far_x = ny - 1 - k // nx, nx - 1 - k % nx
+        return ((x + offset(far_x, nx)) % nx) * ny + (y + offset(far_y, ny)) % ny
 
     def col_peer(k):
-        return (col + k) % nc
+        far_z, far_core = nz - 1 - k // 2, 1 - k % 2
+        return ((z + offset(far_z, nz)) % nz) * 2 + (core + far_core) % 2
 
     def y_peer(k):
         return (x * ny + (y + k) % ny, col)
@@ -72,7 +81,7 @@
                 ).start()
             return carry
 
-        lax.fori_loop(1, nr, go, 0)
+        lax.fori_loop(0, nr - 1, go, 0)
 
     def to_cols(*copies):
         for src_of, dst, send, recv in copies:
@@ -87,7 +96,7 @@
                 ).start()
             return carry
 
-        lax.fori_loop(1, nc, go, 0)
+        lax.fori_loop(0, nc - 1, go, 0)
 
     loads = [pltpu.make_async_copy(a, b, in_sem.at[n]) for n, (a, b) in enumerate((
         (points_in, points), (inv_in, inv), (targets_in, targets), (seeds_in, seeds),
@@ -106,7 +115,7 @@
 
     lax.fori_loop(1, ny, greet(y_peer), 0)
     lax.fori_loop(1, nx, greet(x_peer), 0)
-    lax.fori_loop(1, nc, greet(lambda k: (row, col_peer(k))), 0)
+    lax.fori_loop(0, nc - 1, greet(lambda k: (row, col_peer(k))), 0)
 
     sub = lax.broadcasted_iota(jnp.int32, (RHS, LANES), 0)
     lane = lax.broadcasted_iota(jnp.int32, (RHS, LANES), 1)
@@ -293,8 +302,8 @@
     alpha2 = rr1 / curve2
     d2 = r1 + beta * v0
     image2 = (q1 - alpha1 * q2) + beta * q1
-    sol[...] = alpha1 * v0 + alpha2 * d2
-    res[...] = r1 - alpha2 * image2
+    both[0] = alpha1 * v0 + alpha2 * d2
+    both[1] = r1 - alpha2 * image2
 
 
 def solution(mesh):
@@ -306,14 +315,14 @@
     dma = pltpu.SemaphoreType.DMA
 
     def shards(points, inv_scale, amplitude, noise, targets, probe_seeds):
-        out = jax.ShapeDtypeStruct((RHS, LANES), F32)
+        out = jax.ShapeDtypeStruct((2, RHS, LANES), F32)
         line = pltpu.VMEM((1, LANES), F32)
         plane = pltpu.VMEM((RHS, LANES), F32)
-        return pl.pallas_call(
+        pair = pl.pallas_call(
             lambda *refs: body(nx, ny, nc, refs),
-            out_shape=(out, out),
+            out_shape=out,
             in_specs=[anywhere] * 6,
-            out_specs=(vmem, vmem),
+            out_specs=vmem,
             scratch_shapes=[
                 pltpu.VMEM((F, LANES), BF16), pltpu.VMEM((1, F), F32), pltpu.VMEM((1, 1), F32),
                 line, line, pltpu.VMEM((1, LANES), jnp.int32),
@@ -335,6 +344,7 @@
                 collective_id=0, has_side_effects=True, vmem_limit_bytes=48 * 2**20),
         )(points, inv_scale.reshape(1, F), amplitude.reshape(1, 1), noise.reshape(1, LANES),
           targets.reshape(1, LANES), probe_seeds.reshape(1, LANES))
+        return pair[0], pair[1]
 
     spec = P(("row", "col"))
     both = P(None, ("row", "col"))

time: 57.6 us -> 56 us (0.972)
  Pallas kernels: 54.3 us -> 53.2 us
  local copies, waits for them, and re-layouts: 1.85 us -> 1.26 us
    unnamed x12 -> x10, local copies, waits for them, and re-layouts: 1.85 us -> 0.66 us
    pallas_call x1, Pallas kernels: 54.3 us -> 53.2 us  [shards(): pl.pallas_call(lambda *refs: body(nx, ny, nc, refs), out_shape=out, in_sp...]
    squeeze x0 -> x1, local copies, waits for them, and re-layouts: none -> 0.6 us  [shards(): return (pair[0], pair[1])]
where the time goes in v4:
time: 56 us; the launch traced here: 55.8 us
  Pallas kernels  53.2 us (95%)
  between operations  1.35 us (2%)
  local copies, waits for them, and re-layouts  1.26 us (2%)
    pallas_call x1, Pallas kernels, shards(): pl.pallas_call(lambda *refs: body(nx, ny, nc, refs), out_shape=out, in_sp...  53.2 us

profile of v4, /device:TPU:1, one launch (start us, length us, event | category | flops | bytes accessed | tf_op | source)
XLA Modules:
  0.0 55.8 jit_solution(12692312844514738095)
XLA Ops:
  0.6 0.0 copy-start
  1.3 0.0 copy-start.4
  1.3 0.0 copy-start.1
  1.3 0.0 copy-start.2
  1.3 0.0 copy-start.3
  1.3 0.0 copy-done
  1.3 0.6 %copy-done.4 = s32[128]{0:T(128)S(1)} copy-done((s32[128]{0:T(128)S(1)}, s32[128]{0:T(128)}, u32[]{:S(2)}) %copy-start.4) | copy-done | bytes 536
  2.0 0.0 copy-done.1
  2.0 0.0 copy-done.2
  2.0 0.0 copy-done.3
  2.0 53.2 %shard_map.77 = f32[2,8,128]{2,1,0:T(8,128)S(1)} custom-call(bf16[32,128]{1,0:T(8,128)(2,1)S(1)} %copy-done, f32[1,32]{1,0:T(1,128)S(1)} %bitcast.10, f32[1,1]{1,0:T(1,128)} %bitcast.9.refs_2_, f32[1,128]{1,0:T(1,128)S(1)} %bitcast.11, f32[1,128]{1,0:T(1,128)S(1)} %bitcast.12, s32[1,128]{1,0:T(1,128)S(1)} %bitcast.13), custom_call_target="tpu_custom_call" | custom-call | tf_op jit(solution)/shard_map/pallas_call | solution.py:321
  55.2 0.6 %slice_bitcast_fusion = (f32[8,128]{1,0:T(8,128)}, f32[8,128]{1,0:T(8,128)}) fusion(f32[2,8,128]{2,1,0:T(8,128)S(1)} %shard_map.77), kind=kLoop, calls=%fused_computation | loop fusion | bytes 16384 | tf_op jit(solution)/shard_map/squeeze | solution.py:347
Async XLA Ops:
  0.6 0.7 %copy-start = (bf16[32,128]{1,0:T(8,128)(2,1)S(1)}, bf16[32,128]{1,0:T(8,128)(2,1)}, u32[]{:S(2)}) copy-start(bf16[32,128]{1,0:T(8,128)(2,1)} %refs_0_.1) | copy-start | bytes 24580
  1.3 0.7 %copy-start.4 = (s32[128]{0:T(128)S(1)}, s32[128]{0:T(128)}, u32[]{:S(2)}) copy-start(s32[128]{0:T(128)} %param.11) | copy-start | bytes 1540
  1.3 0.7 %copy-start.1 = (f32[32]{0:T(128)S(1)}, f32[32]{0:T(128)}, u32[]{:S(2)}) copy-start(f32[32]{0:T(128)} %param.7) | copy-start | bytes 388
  1.3 0.7 %copy-start.2 = (f32[128]{0:T(128)S(1)}, f32[128]{0:T(128)}, u32[]{:S(2)}) copy-start(f32[128]{0:T(128)} %param.9) | copy-start | bytes 1540
  1.3 0.7 %copy-start.3 = (f32[128]{0:T(128)S(1)}, f32[128]{0:T(128)}, u32[]{:S(2)}) copy-start(f32[128]{0:T(128)} %param.10) | copy-start | bytes 1540

commit v5 on v4

--- a/solution.py
+++ b/solution.py
@@ -58,6 +58,14 @@
         far_z, far_core = nz - 1 - k // 2, 1 - k % 2
         return ((z + offset(far_z, nz)) % nz) * 2 + (core + far_core) % 2
 
+    def row_peer_x(k):
+        far_x, far_y = nx - 1 - k // ny, ny - 1 - k % ny
+        return ((x + offset(far_x, nx)) % nx) * ny + (y + offset(far_y, ny)) % ny
+
+    def row_peer_n(k):
+        near_x, near_y = (k + 1) // ny, (k + 1) % ny
+        return ((x + nx - turn(near_x)) % nx) * ny + (y + near_y) % ny
+
     def y_peer(k):
         return (x * ny + (y + k) % ny, col)
 
@@ -68,12 +76,12 @@
         half = t // 2 + 1
         return half + (t % 2) * (ny - 2 * half)
 
-    def to_rows(*copies):
+    def to_rows(*copies, peer_of=row_peer):
         for src, dst, send, recv in copies:
             pltpu.make_async_copy(src, dst, recv).start()
 
         def go(k, carry):
-            peer = row_peer(k)
+            peer = peer_of(k)
             for src, dst, send, recv in copies:
                 pltpu.make_async_remote_copy(
                     src_ref=src, dst_ref=dst, send_sem=send, recv_sem=recv,
@@ -149,7 +157,7 @@
     aux[1:2, :] = seeds[...].astype(F32)
 
     pl.semaphore_wait(barrier, ny - 1 + nx - 1 + nc - 1)
-    to_cols((lambda peer: aux, ia.at[col], s_ac, r_ac), (lambda peer: pts, ip.at[col], s_pc, r_pc))
+    to_cols((lambda peer: pts, ip.at[col], s_pc, r_pc))
 
     def copy_to(device, src, dst, send, recv):
         pltpu.make_async_remote_copy(
@@ -175,6 +183,7 @@
     ja[row] = aux[...]
     jp[row] = pts[...]
     forward(row)
+    to_cols((lambda peer: aux, ia.at[col], s_ac, r_ac))
 
     def pass_on(t, carry):
         source = (y + near(t)) % ny
@@ -191,7 +200,6 @@
     shift = noise[...]
     acc[...] = jnp.zeros_like(acc)
 
-    wait_bytes(ia, r_ac)
     wait_bytes(ip, r_pc)
     for c in range(nc):
         part = slice(c * LANES, (c + 1) * LANES)
@@ -200,7 +208,6 @@
         weights[0:F, part] = block
         extra = jnp.where(sub < 3, 1.0, jnp.where(sub == 3, n1, jnp.where(sub == 4, n2, jnp.where(sub == 5, n3, 0.0))))
         weights[F:ROWS, part] = jnp.concatenate([extra, jnp.zeros_like(extra)], axis=0).astype(BF16)
-        v_i[:, part] = build_rhs(ia[c, 0:1], ia[c, 1:2])
 
     def first_pass(t, carry):
         g = (x + turn(t)) % nx
@@ -230,6 +237,9 @@
 
     to_cols((lambda peer: acc.at[pl.ds(RHS, RHS), pl.ds(pl.multiple_of(peer * LANES, LANES), LANES)],
              rs1.at[col], s_rs1, r_rs1))
+    wait_bytes(ia, r_ac)
+    for c in range(nc):
+        v_i[:, c * LANES:(c + 1) * LANES] = build_rhs(ia[c, 0:1], ia[c, 1:2])
     low_i = v_i[...].astype(BF16).astype(F32)
     s1_msg[...] = as_row((
         rowsum(v0 * v0), scale * rowsum(low_i * acc[RHS:2 * RHS, :]) + rowsum(shift * low * low)))
@@ -311,7 +321,7 @@
     ny = 8 if nr % 8 == 0 else nr
     nx = nr // ny
     vmem = pl.BlockSpec(memory_space=pltpu.VMEM)
-    anywhere = pl.BlockSpec(memory_space=pl.ANY)
+    anywhere = pl.BlockSpec(memory_space=pltpu.HBM)
     dma = pltpu.SemaphoreType.DMA
 
     def shards(points, inv_scale, amplitude, noise, targets, probe_seeds):

time: 56 us -> 55.8 us (level)
  no operation moved by 1% of the time
where the time goes in v5:
time: 55.8 us; the launch traced here: 55.6 us
  Pallas kernels  53 us (95%)
  between operations  1.35 us (2%)
  local copies, waits for them, and re-layouts  1.26 us (2%)
    pallas_call x1, Pallas kernels, shards(): pl.pallas_call(lambda *refs: body(nx, ny, nc, refs), out_shape=out, in_sp...  53 us

profile of v5, /device:TPU:1, one launch (start us, length us, event | category | flops | bytes accessed | tf_op | source)
XLA Modules:
  0.0 55.6 jit_solution(17444085221335760465)
XLA Ops:
  0.6 0.0 copy-start
  1.3 0.0 copy-start.4
  1.3 0.0 copy-start.1
  1.3 0.0 copy-start.2
  1.3 0.0 copy-start.3
  1.3 0.0 copy-done
  1.3 0.6 %copy-done.4 = s32[128]{0:T(128)S(1)} copy-done((s32[128]{0:T(128)S(1)}, s32[128]{0:T(128)}, u32[]{:S(2)}) %copy-start.4) | copy-done | bytes 536
  2.0 0.0 copy-done.1
  2.0 0.0 copy-done.2
  2.0 0.0 copy-done.3
  2.0 53.0 %shard_map.77 = f32[2,8,128]{2,1,0:T(8,128)S(1)} custom-call(bf16[32,128]{1,0:T(8,128)(2,1)S(1)} %copy-done, f32[1,32]{1,0:T(1,128)S(1)} %bitcast.10, f32[1,1]{1,0:T(1,128)} %bitcast.9.refs_2_, f32[1,128]{1,0:T(1,128)S(1)} %bitcast.11, f32[1,128]{1,0:T(1,128)S(1)} %bitcast.12, s32[1,128]{1,0:T(1,128)S(1)} %bitcast.13), custom_call_target="tpu_custom_call" | custom-call | tf_op jit(solution)/shard_map/pallas_call | solution.py:331
  55.0 0.6 %slice_bitcast_fusion = (f32[8,128]{1,0:T(8,128)}, f32[8,128]{1,0:T(8,128)}) fusion(f32[2,8,128]{2,1,0:T(8,128)S(1)} %shard_map.77), kind=kLoop, calls=%fused_computation | loop fusion | bytes 16384 | tf_op jit(solution)/shard_map/squeeze | solution.py:357
Async XLA Ops:
  0.6 0.7 %copy-start = (bf16[32,128]{1,0:T(8,128)(2,1)S(1)}, bf16[32,128]{1,0:T(8,128)(2,1)}, u32[]{:S(2)}) copy-start(bf16[32,128]{1,0:T(8,128)(2,1)} %refs_0_.1) | copy-start | bytes 24580
  1.3 0.7 %copy-start.4 = (s32[128]{0:T(128)S(1)}, s32[128]{0:T(128)}, u32[]{:S(2)}) copy-start(s32[128]{0:T(128)} %param.11) | copy-start | bytes 1540
  1.3 0.7 %copy-start.1 = (f32[32]{0:T(128)S(1)}, f32[32]{0:T(128)}, u32[]{:S(2)}) copy-start(f32[32]{0:T(128)} %param.7) | copy-start | bytes 388
  1.3 0.7 %copy-start.2 = (f32[128]{0:T(128)S(1)}, f32[128]{0:T(128)}, u32[]{:S(2)}) copy-start(f32[128]{0:T(128)} %param.9) | copy-start | bytes 1540
  1.3 0.7 %copy-start.3 = (f32[128]{0:T(128)S(1)}, f32[128]{0:T(128)}, u32[]{:S(2)}) copy-start(f32[128]{0:T(128)} %param.10) | copy-start | bytes 1540

commit v6 on v5

--- a/solution.py
+++ b/solution.py
@@ -89,7 +89,7 @@
                 ).start()
             return carry
 
-        lax.fori_loop(0, nr - 1, go, 0)
+        lax.fori_loop(0, nr - 1, go, 0, unroll=True)
 
     def to_cols(*copies):
         for src_of, dst, send, recv in copies:
@@ -104,7 +104,7 @@
                 ).start()
             return carry
 
-        lax.fori_loop(0, nc - 1, go, 0)
+        lax.fori_loop(0, nc - 1, go, 0, unroll=True)
 
     loads = [pltpu.make_async_copy(a, b, in_sem.at[n]) for n, (a, b) in enumerate((
         (points_in, points), (inv_in, inv), (targets_in, targets), (seeds_in, seeds),

time: 55.8 us -> 55 us (0.986)
  Pallas kernels: 53 us -> 52.2 us
    pallas_call x1, Pallas kernels: 53 us -> 52.2 us  [shards(): pl.pallas_call(lambda *refs: body(nx, ny, nc, refs), out_shape=out, in_sp...]
where the time goes in v6:
time: 55 us; the launch traced here: 54.8 us
  Pallas kernels  52.2 us (95%)
  between operations  1.35 us (2%)
  local copies, waits for them, and re-layouts  1.26 us (2%)
    pallas_call x1, Pallas kernels, shards(): pl.pallas_call(lambda *refs: body(nx, ny, nc, refs), out_shape=out, in_sp...  52.2 us

profile of v6, /device:TPU:1, one launch (start us, length us, event | category | flops | bytes accessed | tf_op | source)
XLA Modules:
  0.0 54.8 jit_solution(9099620274460610745)
XLA Ops:
  0.6 0.0 copy-start
  1.3 0.0 copy-start.4
  1.3 0.0 copy-start.1
  1.3 0.0 copy-start.2
  1.3 0.0 copy-start.3
  1.3 0.0 copy-done
  1.3 0.6 %copy-done.4 = s32[128]{0:T(128)S(1)} copy-done((s32[128]{0:T(128)S(1)}, s32[128]{0:T(128)}, u32[]{:S(2)}) %copy-start.4) | copy-done | bytes 536
  2.0 0.0 copy-done.1
  2.0 0.0 copy-done.2
  2.0 0.0 copy-done.3
  2.0 52.2 %shard_map.77 = f32[2,8,128]{2,1,0:T(8,128)S(1)} custom-call(bf16[32,128]{1,0:T(8,128)(2,1)S(1)} %copy-done, f32[1,32]{1,0:T(1,128)S(1)} %bitcast.10, f32[1,1]{1,0:T(1,128)} %bitcast.9.refs_2_, f32[1,128]{1,0:T(1,128)S(1)} %bitcast.11, f32[1,128]{1,0:T(1,128)S(1)} %bitcast.12, s32[1,128]{1,0:T(1,128)S(1)} %bitcast.13), custom_call_target="tpu_custom_call" | custom-call | tf_op jit(solution)/shard_map/pallas_call | solution.py:331
  54.2 0.6 %slice_bitcast_fusion = (f32[8,128]{1,0:T(8,128)}, f32[8,128]{1,0:T(8,128)}) fusion(f32[2,8,128]{2,1,0:T(8,128)S(1)} %shard_map.77), kind=kLoop, calls=%fused_computation | loop fusion | bytes 16384 | tf_op jit(solution)/shard_map/squeeze | solution.py:357
Async XLA Ops:
  0.6 0.7 %copy-start = (bf16[32,128]{1,0:T(8,128)(2,1)S(1)}, bf16[32,128]{1,0:T(8,128)(2,1)}, u32[]{:S(2)}) copy-start(bf16[32,128]{1,0:T(8,128)(2,1)} %refs_0_.1) | copy-start | bytes 24580
  1.3 0.7 %copy-start.4 = (s32[128]{0:T(128)S(1)}, s32[128]{0:T(128)}, u32[]{:S(2)}) copy-start(s32[128]{0:T(128)} %param.11) | copy-start | bytes 1540
  1.3 0.7 %copy-start.1 = (f32[32]{0:T(128)S(1)}, f32[32]{0:T(128)}, u32[]{:S(2)}) copy-start(f32[32]{0:T(128)} %param.7) | copy-start | bytes 388
  1.3 0.7 %copy-start.2 = (f32[128]{0:T(128)S(1)}, f32[128]{0:T(128)}, u32[]{:S(2)}) copy-start(f32[128]{0:T(128)} %param.9) | copy-start | bytes 1540
  1.3 0.7 %copy-start.3 = (f32[128]{0:T(128)S(1)}, f32[128]{0:T(128)}, u32[]{:S(2)}) copy-start(f32[128]{0:T(128)} %param.10) | copy-start | bytes 1540
